TPU v7x, 32 devices: a whole 2x2x4 slice. The times are simulated.
32 devices in a mesh: cfg: 2 (over core), tower: 4 (over z), seq: 4 (over y, x).
Axes of the slice: x: 2, y: 2, z: 4, core: 2. Of those that a mesh axis runs over, the one named last changes fastest.
Arguments:
- query_self: bfloat16 [2, 256, 2048], P('cfg', ('tower', 'seq')), may hold values from -320 to 320
- query_cross: bfloat16 [2, 256, 2048], P('cfg', ('tower', 'seq')), may hold values from -320 to 320
- key_vectors: bfloat16 [2, 256, 2048], P('cfg', ('tower', 'seq')), may hold values from -13 to 13
- values: bfloat16 [2, 256, 2048], P('cfg', ('tower', 'seq')), may hold values from -6 to 6
- positions: int32 [256], P(('tower', 'seq')), may hold values from 0 to 155, as said below
- counts: int32 [16], replicated, may hold values from 8 to 16, as said below
- guidance: float32 [1], replicated, may hold values from 1.5 to 3.5
Outputs:
- guided: bfloat16 [256, 2048], P(('tower', 'seq'), 'cfg')
Inputs may be any that keep to these rules, and one draw needn't show every extreme that they name: `positions`: integer times on one clock for video and audio tokens, never falling along the video tokens and along the audio tokens; the video tokens of one latent frame share a time. `counts`: valid tokens of each device; a device's slots beyond its count are padding.
All inputs are finite; a program needn't handle non-finite values.
Results may differ from a plain program's by a relative error of at most 0.029.
Values may be sent and summed in bfloat16 or wider, within the bound.
No kernel may reach another device: no remote copies, remote signals or barrier semaphores. Data moves between devices by JAX's collectives and lax.ppermute only.
A program may use at most 64 MiB of HBM per device.

v0:
```python
import math

import jax
import jax.numpy as jnp
from jax import lax
from jax.sharding import PartitionSpec as P

HEADS = 16
DHEAD = 128


def rotate_heads(matrix, positions):
    token_count = matrix.shape[0]
    half_dim = DHEAD // 2
    frequency = 10000.0 ** (-(jnp.arange(half_dim, dtype=jnp.float32) * 2.0 / DHEAD))
    angles = positions.astype(jnp.float32)[:, None] * frequency[None, :]
    cosine = jnp.cos(angles)[:, None, :]
    sine_part = jnp.sin(angles)[:, None, :]
    heads_f32 = matrix.astype(jnp.float32).reshape(token_count, HEADS, DHEAD)
    front_half = heads_f32[..., :half_dim]
    back_half = heads_f32[..., half_dim:]
    rotated = jnp.concatenate(
        [front_half * cosine - back_half * sine_part, back_half * cosine + front_half * sine_part],
        axis=-1,
    )
    return rotated.reshape(token_count, HEADS * DHEAD).astype(jnp.bfloat16)


def attend_blocks(queries, key_rows, value_rows, key_mask, key_block):
    query_count, per_dev, head_dim = queries.shape
    piece_count = key_rows.shape[0] // key_block
    key_pieces = key_rows.reshape(piece_count, key_block, per_dev, head_dim)
    value_pieces = value_rows.reshape(piece_count, key_block, per_dev, head_dim)
    mask_pieces = key_mask.reshape(piece_count, key_block)
    scale_factor = 1.0 / math.sqrt(head_dim)
    start_state = (
        jnp.full((per_dev, query_count), -1e30, jnp.float32),
        jnp.zeros((per_dev, query_count), jnp.float32),
        jnp.zeros((per_dev, query_count, head_dim), jnp.float32),
    )

    def advance(running, pieces):
        highest, weight_sum, weighted = running
        key_piece, value_piece, mask_piece = pieces
        scores = (
            jnp.einsum("qhd,khd->hqk", queries, key_piece, preferred_element_type=jnp.float32)
            * scale_factor
        )
        scores = jnp.where(mask_piece[None, None, :], scores, -1e30)
        new_high = jnp.maximum(highest, jnp.max(scores, axis=2))
        weights = jnp.where(mask_piece[None, None, :], jnp.exp(scores - new_high[:, :, None]), 0.0)
        factor = jnp.exp(highest - new_high)
        weight_sum = weight_sum * factor + jnp.sum(weights, axis=2)
        weighted = weighted * factor[:, :, None] + jnp.einsum(
            "hqk,khd->hqd",
            weights.astype(jnp.bfloat16),
            value_piece,
            preferred_element_type=jnp.float32,
        )
        return ((new_high, weight_sum, weighted), None)

    final_state, ignored = lax.scan(advance, start_state, (key_pieces, value_pieces, mask_pieces))
    return final_state


def per_device(query_self, query_cross, key_vectors, values, positions, counts, guidance):
    n_seq = lax.axis_size("seq")
    n_tower = lax.axis_size("tower")
    tokens_here = query_self.shape[1]
    feature_count = query_self.shape[2]
    per_dev = max(HEADS // n_seq, 1)
    query_blocks = max(n_seq // HEADS, 1)
    groups = HEADS // per_dev
    head_width = per_dev * DHEAD
    block_rows = tokens_here // query_blocks
    key_block = tokens_here * min(n_seq, 16)
    tower_at = lax.axis_index("tower")
    seq_at = lax.axis_index("seq")
    is_audio = tower_at == n_tower - 1
    rot_self = rotate_heads(query_self[0], positions)
    rot_cross = rotate_heads(query_cross[0], positions)
    rot_keys = rotate_heads(key_vectors[0], positions)
    value_rows = values[0]
    count_table = counts.reshape(n_tower, n_seq)
    slot_valid = jnp.arange(tokens_here, dtype=jnp.int32)[None, None, :] < count_table[:, :, None]
    key_valid = slot_valid.reshape(n_tower, n_seq * tokens_here)

    def spread_queries(matrix):
        parts = matrix.reshape(query_blocks, block_rows, groups, head_width).transpose(2, 0, 1, 3)
        return parts.reshape(n_seq, 1, block_rows, head_width)

    def spread_keys(matrix, towers_here):
        parts = matrix.reshape(towers_here, tokens_here, groups, head_width).transpose(2, 0, 1, 3)
        parts = jnp.broadcast_to(
            parts[:, None], (groups, query_blocks, towers_here, tokens_here, head_width)
        )
        return parts.reshape(n_seq, towers_here, tokens_here, head_width)

    key_source, value_source = (
        lax.all_gather(rot_keys, "tower", axis=0, tiled=True),
        lax.all_gather(value_rows, "tower", axis=0, tiled=True),
    )
    towers_here = n_tower
    arrived = (
        lax.all_to_all(spread_queries(rot_self), "seq", split_axis=0, concat_axis=2, tiled=True),
        lax.all_to_all(spread_queries(rot_cross), "seq", split_axis=0, concat_axis=2, tiled=True),
        lax.all_to_all(
            spread_keys(key_source, towers_here), "seq", split_axis=0, concat_axis=2, tiled=True
        ),
        lax.all_to_all(
            spread_keys(value_source, towers_here), "seq", split_axis=0, concat_axis=2, tiled=True
        ),
    )
    query_count = n_seq * block_rows
    key_count = n_seq * tokens_here
    head_self = arrived[0].reshape(query_count, per_dev, DHEAD)
    head_cross = arrived[1].reshape(query_count, per_dev, DHEAD)
    key_all = arrived[2].reshape(n_tower, key_count, per_dev, DHEAD)
    value_all = arrived[3].reshape(n_tower, key_count, per_dev, DHEAD)
    video_query = jnp.where(is_audio, head_cross, head_self)
    audio_query = jnp.where(is_audio, head_self, head_cross)
    video_count = (n_tower - 1) * key_count
    video_state = attend_blocks(
        video_query,
        key_all[: n_tower - 1].reshape(video_count, per_dev, DHEAD),
        value_all[: n_tower - 1].reshape(video_count, per_dev, DHEAD),
        key_valid[: n_tower - 1].reshape(video_count),
        key_block,
    )
    audio_state = attend_blocks(
        audio_query, key_all[n_tower - 1], value_all[n_tower - 1], key_valid[n_tower - 1], key_block
    )
    combined = (
        video_state[2] / video_state[1][:, :, None] + audio_state[2] / audio_state[1][:, :, None]
    )
    block_heads = (
        combined.transpose(1, 0, 2).reshape(n_seq, block_rows, head_width).astype(jnp.bfloat16)
    )
    returned = lax.all_to_all(block_heads, "seq", split_axis=0, concat_axis=0, tiled=True)
    token_major = (
        returned.reshape(groups, query_blocks, block_rows, head_width)
        .transpose(1, 2, 0, 3)
        .reshape(tokens_here, feature_count)
    )
    own_count = count_table[tower_at, seq_at]
    own_valid = jnp.arange(tokens_here, dtype=jnp.int32) < own_count
    block_rows_kept = jnp.where(own_valid[:, None], token_major, jnp.zeros_like(token_major))
    block_f32 = block_rows_kept.astype(jnp.float32)
    scale_rows = lax.rsqrt(jnp.mean(block_f32 * block_f32, axis=1, keepdims=True) + 1e-06)
    normed = (block_f32 * scale_rows).astype(jnp.bfloat16)
    paired = lax.all_to_all(normed[None], "cfg", split_axis=2, concat_axis=0, tiled=True)
    conditional = paired[0].astype(jnp.float32)
    unconditional = paired[1].astype(jnp.float32)
    return (unconditional + guidance[0] * (conditional - unconditional)).astype(jnp.bfloat16)


def solution(mesh):
    return jax.shard_map(
        per_device,
        mesh=mesh,
        in_specs=(
            P("cfg", ("tower", "seq"), None),
            P("cfg", ("tower", "seq"), None),
            P("cfg", ("tower", "seq"), None),
            P("cfg", ("tower", "seq"), None),
            P(("tower", "seq")),
            P(),
            P(),
        ),
        out_specs=P(("tower", "seq"), "cfg"),
        check_vma=False,
    )
```

profile of v0, /device:TPU:0, one launch (start us, length us, event | category | flops | bytes accessed | tf_op | source)
XLA Modules:
  0.0 95.0 jit_solution(3552296295865331659)
XLA Ops:
  0.0 0.6 copy-done.5
  0.7 0.8 convert_bitcast_fusion.2
  1.6 0.8 copy-done
  2.4 0.8 copy-done.1
  3.7 0.6 copy.58
  4.4 5.2 %all-to-all-start.1 = ((bf16[4,1,16,512]{3,2,1,0:T(8,128)(2,1)}), bf16[4,1,16,512]{3,2,1,0:T(8,128)(2,1)S(1)}, u32[]{:S(2)}, u32[]{:S(2)}) async-start(bf16[4,1,16,512]{3,2,1,0:T(8,128)(2,1)} %copy.58), calls=%async_computation.1 | async-start | bytes 131072 | tf_op jit(solution)/shard_map/all_to_all | solution.py:106
  9.7 0.6 copy.59
  10.3 4.1 %all-to-all-done.1 = bf16[4,1,16,512]{3,2,1,0:T(8,128)(2,1)S(1)} async-done(((bf16[4,1,16,512]{3,2,1,0:T(8,128)(2,1)}), bf16[4,1,16,512]{3,2,1,0:T(8,128)(2,1)S(1)}, u32[]{:S(2)}, u32[]{:S(2)}) %all-to-all-start.1) | async-done | bytes 65568 | tf_op jit(solution)/shard_map/all_to_all | solution.py:106
  14.4 3.3 %all-to-all-start.2 = ((bf16[4,1,16,512]{3,2,1,0:T(8,128)(2,1)}), bf16[4,1,16,512]{3,2,1,0:T(8,128)(2,1)S(1)}, u32[]{:S(2)}, u32[]{:S(2)}) async-start(bf16[4,1,16,512]{3,2,1,0:T(8,128)(2,1)} %copy.59), calls=%async_computation.2 | async-start | bytes 131072 | tf_op jit(solution)/shard_map/all_to_all | solution.py:105
  17.7 14.1 %all_gather.6 = bf16[64,2048]{1,0:T(8,128)(2,1)S(1)} all-gather(bf16[16,2048]{1,0:T(8,128)(2,1)S(1)} %bitcast.99), channel_id=1, replica_groups=mesh['cfg'=2,'tower'=4,'seq'=4] {'tower'}, dimensions={0}, use_global_device_ids=true | all-gather | bytes 327680 | tf_op jit(solution)/shard_map/all_gather | solution.py:100
  32.0 0.7 copy.56
  32.8 4.5 %all-to-all-start = ((bf16[4,4,16,512]{3,2,1,0:T(8,128)(2,1)}), bf16[4,4,16,512]{3,2,1,0:T(8,128)(2,1)S(1)}, u32[]{:S(2)}, u32[]{:S(2)}) async-start(bf16[4,4,16,512]{3,2,1,0:T(8,128)(2,1)} %copy.56), calls=%async_computation | async-start | bytes 524288 | tf_op jit(solution)/shard_map/all_to_all | solution.py:107
  37.4 0.6 copy-done.3
  38.0 0.7 slice-done
  38.8 13.9 %all-gather = bf16[1,64,2048]{2,1,0:T(8,128)(2,1)S(1)} all-gather(bf16[1,16,2048]{2,1,0:T(8,128)(2,1)S(1)} %copy-done.2), channel_id=2, replica_groups=mesh['cfg'=2,'tower'=4,'seq'=4] {'tower'}, dimensions={1}, use_global_device_ids=true | all-gather | bytes 327680 | tf_op jit(solution)/shard_map/all_gather | solution.py:101
  52.9 0.8 copy.60
  53.7 0.6 dynamic_slice.22
  54.3 4.1 %all-to-all-start.3 = ((bf16[4,4,16,512]{3,2,1,0:T(8,128)(2,1)}), bf16[4,4,16,512]{3,2,1,0:T(8,128)(2,1)S(1)}, u32[]{:S(2)}, u32[]{:S(2)}) async-start(bf16[4,4,16,512]{3,2,1,0:T(8,128)(2,1)} %copy.60), calls=%async_computation.3 | async-start | bytes 524288 | tf_op jit(solution)/shard_map/all_to_all | solution.py:110
  58.5 5.2 %all-to-all-done.3 = bf16[4,4,16,512]{3,2,1,0:T(8,128)(2,1)S(1)} async-done(((bf16[4,4,16,512]{3,2,1,0:T(8,128)(2,1)}), bf16[4,4,16,512]{3,2,1,0:T(8,128)(2,1)S(1)}, u32[]{:S(2)}, u32[]{:S(2)}) %all-to-all-start.3) | async-done | bytes 262176 | tf_op jit(solution)/shard_map/all_to_all | solution.py:110
  64.2 2.2 %while.3 = (s32[]{:T(128)}, f32[4,64]{1,0:T(4,128)S(1)}, f32[4,64]{1,0:T(4,128)S(1)}, f32[4,64,128]{2,1,0:T(8,128)S(1)}, pred[3,64]{1,0:T(4,128)(4,1)S(1)}, /*in...) while((s32[]{:T(128)}, f32[4,64]{1,0:T(4,128)S(1)}, ...), condition=%wide.region_3.4_spmd.clone, body=%wide.region_0.3_spmd.clone.sunk | while | flops 8635651 | bytes 934329 | solution.py:62
  66.8 0.7 convert_element_type.119
  67.4 3.3 %all-to-all-start.4 = ((bf16[4,16,512]{2,1,0:T(8,128)(2,1)}), bf16[4,16,512]{2,1,0:T(8,128)(2,1)S(1)}, u32[]{:S(2)}, u32[]{:S(2)}) async-start(bf16[4,16,512]{2,1,0:T(8,128)(2,1)} %convert_element_type.119), calls=%async_computation.4 | async-start | bytes 131072 | tf_op jit(solution)/shard_map/all_to_all | solution.py:139
  70.7 0.7 iota_compare_fusion.1
  72.0 3.5 %all-to-all-done.4 = bf16[4,16,512]{2,1,0:T(8,128)(2,1)S(1)} async-done(((bf16[4,16,512]{2,1,0:T(8,128)(2,1)}), bf16[4,16,512]{2,1,0:T(8,128)(2,1)S(1)}, u32[]{:S(2)}, u32[]{:S(2)}) %all-to-all-start.4) | async-done | bytes 65568 | tf_op jit(solution)/shard_map/all_to_all | solution.py:139
  75.9 0.7 copy.71
  76.6 0.5 broadcast.202
  77.1 11.5 %reduce.1 = bf16[2048,16]{1,0:T(8,128)(2,1)S(1)} reduce(bf16[2048,1,16]{2,1,0:T(2,128)(2,1)S(1)} %bitcast.86, bf16[]{:T(256)} %broadcast.202), dimensions={1}, to_apply=%bitcast.71.reduce_sub_computation | reduce | bytes 131074
  88.7 0.5 reshape.253
  89.2 3.8 %all_to_all.68 = bf16[2,2,8192]{2,1,0:T(2,128)(2,1)S(1)} all-to-all(bf16[2,2,8192]{2,1,0:T(2,128)(2,1)S(1)} %reshape.253), channel_id=1, replica_groups=mesh['cfg'=2,'tower'=4,'seq'=4] {'cfg'}, dimensions={0} | all-to-all | bytes 131072 | tf_op jit(solution)/shard_map/all_to_all | solution.py:151
  93.0 0.8 reshape.254
  93.8 0.5 copy.72
  94.4 0.6 fusion.18
  (86 shorter events, 4.8 us)
Async XLA Ops:
  0.0 0.7 copy-start.5
  1.5 0.8 copy-start
  2.4 0.8 copy-start.1
  4.4 10.0 %all-to-all-start.1 = ((bf16[4,1,16,512]{3,2,1,0:T(8,128)(2,1)}), bf16[4,1,16,512]{3,2,1,0:T(8,128)(2,1)S(1)}, u32[]{:S(2)}, u32[]{:S(2)}) async-start(bf16[4,1,16,512]{3,2,1,0:T(8,128)(2,1)} %copy.58), calls=%async_computation.1 | async-start | bytes 131072 | tf_op jit(solution)/shard_map/all_to_all | solution.py:106
  14.4 18.5 %all-to-all-start.2 = ((bf16[4,1,16,512]{3,2,1,0:T(8,128)(2,1)}), bf16[4,1,16,512]{3,2,1,0:T(8,128)(2,1)S(1)}, u32[]{:S(2)}, u32[]{:S(2)}) async-start(bf16[4,1,16,512]{3,2,1,0:T(8,128)(2,1)} %copy.59), calls=%async_computation.2 | async-start | bytes 131072 | tf_op jit(solution)/shard_map/all_to_all | solution.py:105
  32.0 0.8 copy-start.4
  32.8 6.0 %copy-start.2 = (bf16[1,16,2048]{2,1,0:T(8,128)(2,1)S(1)}, bf16[1,16,2048]{2,1,0:T(8,128)(2,1)}, u32[]{:S(2)}) copy-start(bf16[1,16,2048]{2,1,0:T(8,128)(2,1)} %param.12) | copy-start | bytes 196612
  32.8 21.4 %all-to-all-start = ((bf16[4,4,16,512]{3,2,1,0:T(8,128)(2,1)}), bf16[4,4,16,512]{3,2,1,0:T(8,128)(2,1)S(1)}, u32[]{:S(2)}, u32[]{:S(2)}) async-start(bf16[4,4,16,512]{3,2,1,0:T(8,128)(2,1)} %copy.56), calls=%async_computation | async-start | bytes 524288 | tf_op jit(solution)/shard_map/all_to_all | solution.py:107
  37.4 0.6 copy-start.3
  38.0 0.7 slice-start
  38.0 0.7 slice-start.1
  54.3 9.5 %all-to-all-start.3 = ((bf16[4,4,16,512]{3,2,1,0:T(8,128)(2,1)}), bf16[4,4,16,512]{3,2,1,0:T(8,128)(2,1)S(1)}, u32[]{:S(2)}, u32[]{:S(2)}) async-start(bf16[4,4,16,512]{3,2,1,0:T(8,128)(2,1)} %copy.60), calls=%async_computation.3 | async-start | bytes 524288 | tf_op jit(solution)/shard_map/all_to_all | solution.py:110
  67.4 8.1 %all-to-all-start.4 = ((bf16[4,16,512]{2,1,0:T(8,128)(2,1)}), bf16[4,16,512]{2,1,0:T(8,128)(2,1)S(1)}, u32[]{:S(2)}, u32[]{:S(2)}) async-start(bf16[4,16,512]{2,1,0:T(8,128)(2,1)} %convert_element_type.119), calls=%async_computation.4 | async-start | bytes 131072 | tf_op jit(solution)/shard_map/all_to_all | solution.py:139
where the time goes:
time: 95.9 us; the launch traced here: 95 us
  blocking collectives  31.8 us (33%)
  starting transfers between devices  20.3 us (21%)
  other arithmetic  15.2 us (16%)
  waiting for transfers between devices  12.8 us (13%)
  local copies, waits for them, and re-layouts  11.9 us (12%)
  matrix products  1.89 us (2%)
    all_gather x1, blocking collectives, per_device(): lax.all_gather(rot_keys, 'tower', axis=0, tiled=True)  14.1 us
    all_gather x1, blocking collectives, per_device(): lax.all_gather(value_rows, 'tower', axis=0, tiled=True)  13.9 us
    unnamed x7, other arithmetic  12.4 us
    all_to_all x1, waiting for transfers between devices, per_device(): lax.all_to_all(spread_keys(value_source, towers_here), 'seq', split_axis=...  5.25 us
    all_to_all x1, starting transfers between devices, per_device(): lax.all_to_all(spread_queries(rot_cross), 'seq', split_axis=0, concat_axi...  5.16 us
    unnamed x20, local copies, waits for them, and re-layouts  4.76 us
    all_to_all x1, starting transfers between devices, per_device(): lax.all_to_all(spread_keys(key_source, towers_here), 'seq', split_axis=0,...  4.52 us
    all_to_all x1, starting transfers between devices, per_device(): lax.all_to_all(spread_keys(value_source, towers_here), 'seq', split_axis=...  4.09 us
  transfers between devices with their start and end apart: 5, of which 3 were waited for; matrix products, arithmetic and copies ran while one was open for 5% of the time, Pallas kernels for 0%

commit v1 on v0

v1 whole, which is shorter than its diff:
```python
import functools
import math

import jax
import jax.numpy as jnp
from jax import lax
from jax.experimental import pallas as pl
from jax.experimental.pallas import tpu as pltpu
from jax.sharding import PartitionSpec as P

HEADS = 16
DHEAD = 128
EXPONENT_SCALE = math.log2(math.e) / math.sqrt(DHEAD)
VMEM_LIMIT = 32 * 1024 * 1024


def rotate_kernel(video_keys, positions_hbm, counts_hbm, *refs):
    sources, (packed_ref, bias_ref, kept_ref) = refs[:4], refs[4:7]
    held, positions_ref, counts_ref, semaphores = refs[7:]
    tokens = held.shape[1]
    copies = [pltpu.make_async_copy(positions_hbm, positions_ref, semaphores.at[4])]
    for part in range(4):
        copies.append(
            pltpu.make_async_copy(sources[part].at[0], held.at[part], semaphores.at[part])
        )
    copies.append(pltpu.make_async_copy(counts_hbm, counts_ref, semaphores.at[5]))
    for copy in copies:
        copy.start()
    copies[0].wait()
    row = lax.broadcasted_iota(jnp.int32, (tokens, DHEAD), 0)
    lane = lax.broadcasted_iota(jnp.int32, (tokens, DHEAD), 1)
    time = jnp.zeros((tokens, DHEAD), jnp.int32)
    for token in range(tokens):
        time = jnp.where(row == token, positions_ref[token], time)
    half = DHEAD // 2
    index = (lane % half).astype(jnp.float32)
    angles = time.astype(jnp.float32) * jnp.exp(index * (-2.0 * math.log(10000.0) / DHEAD))
    cosine = jnp.cos(angles)
    sine = jnp.where(lane < half, -jnp.sin(angles), jnp.sin(angles))
    for part in range(4):
        copies[1 + part].wait()
        for head in range(HEADS):
            columns = held[part, :, head * DHEAD : (head + 1) * DHEAD]
            if part < 3:
                columns = columns.astype(jnp.float32)
                columns = columns * cosine + pltpu.roll(columns, half, 1) * sine
            packed_ref[head, part] = columns.astype(jnp.bfloat16)
    copies[5].wait()
    devices = counts_ref.shape[0]
    limits = [counts_ref[device] for device in range(devices)]
    key = lax.broadcasted_iota(jnp.int32, bias_ref.shape, 1)
    past = jnp.zeros(bias_ref.shape, jnp.int32)
    for device in range(devices):
        first = device * tokens
        past = jnp.where(key >= first, first + limits[device], past)
    is_audio = (key >= video_keys).astype(jnp.int32)
    modality = lax.broadcasted_iota(jnp.int32, bias_ref.shape, 0)
    bias_ref[...] = jnp.where((key < past) & (is_audio == modality), 0.0, -1e30)
    block_rows = kept_ref.shape[0] // devices
    slot = lax.broadcasted_iota(jnp.int32, (block_rows, DHEAD), 0)
    if block_rows < tokens:
        part = lax.rem(lax.axis_index(("tower", "seq")), tokens // block_rows)
        slot += part * block_rows
    for device in range(devices):
        rows = pl.ds(device * block_rows, block_rows)
        kept_ref[rows, :] = jnp.where(slot < limits[device], 1.0, 0.0)


def attend(queries, keys, values, bias):
    scores = lax.dot_general(
        queries, keys, (((1,), (1,)), ((), ())), preferred_element_type=jnp.float32
    )
    scores = scores + bias
    weights = jnp.exp2((scores - jnp.max(scores, axis=1, keepdims=True)) * EXPONENT_SCALE)
    both = jnp.dot(
        weights.astype(jnp.bfloat16),
        jnp.concatenate([values, jnp.ones_like(values)], axis=1),
        preferred_element_type=jnp.float32,
    )
    return both[:, :DHEAD], both[:, DHEAD:]


def attend_kernel(n_tower, ranks, bias_ref, kept_ref, *refs):
    out_ref = refs[-1]
    devices, block_rows, _ = out_ref.shape
    if len(refs) == 2:
        q_self, q_cross, keys, values = (
            jnp.concatenate([refs[0][rank, part] for rank in ranks[0]], axis=0)
            for part in range(4)
        )
    else:
        q_self, q_cross, keys, values = (ref[...] for ref in refs[:4])
    video_keys = keys.shape[0] // n_tower * (n_tower - 1)
    video_queries = q_self.shape[0] // n_tower * (n_tower - 1)
    to_video = jnp.concatenate([q_self[:video_queries], q_cross[video_queries:]], axis=0)
    to_audio = jnp.concatenate([q_cross[:video_queries], q_self[video_queries:]], axis=0)
    last_video = pl.cdiv(video_keys, DHEAD) * DHEAD
    first_audio = video_keys // DHEAD * DHEAD
    video, video_sum = attend(
        to_video, keys[:last_video], values[:last_video], bias_ref[0:1, :last_video]
    )
    audio, audio_sum = attend(
        to_audio, keys[first_audio:], values[first_audio:], bias_ref[1:2, first_audio:]
    )
    combined = video * audio_sum + audio * video_sum
    combined = (combined * (kept_ref[...] / (video_sum * audio_sum))).astype(jnp.bfloat16)
    for device in range(devices):
        out_ref[ranks[1][device]] = combined[device * block_rows : (device + 1) * block_rows]


def norm_kernel(head_ranks, blocks_ref, kept_ref, sent_ref):
    heads, tokens, _ = blocks_ref.shape
    half_heads = heads // 2
    core = lax.axis_index("cfg")
    total = jnp.zeros((tokens, DHEAD), jnp.float32)
    for head in range(heads):
        block = blocks_ref[head].astype(jnp.float32)
        total += block * block
    mean = jnp.sum(total, axis=1, keepdims=True) * (1.0 / (heads * DHEAD))
    scale = lax.rsqrt(mean + 1e-6)
    for at in range(half_heads):
        low, high = head_ranks[at], head_ranks[half_heads + at]
        for rank, target in (
            (jnp.where(core == 0, low, high), kept_ref),
            (jnp.where(core == 0, high, low), sent_ref),
        ):
            normed = blocks_ref[rank].astype(jnp.float32) * scale
            target[:, at * DHEAD : (at + 1) * DHEAD] = normed.astype(jnp.bfloat16)


def guide_kernel(guidance_ref, kept_ref, met_ref, out_ref):
    kept, met = kept_ref[...].astype(jnp.float32), met_ref[...].astype(jnp.float32)
    first = lax.axis_index("cfg") == 0
    conditional, unconditional = jnp.where(first, kept, met), jnp.where(first, met, kept)
    guided = unconditional + guidance_ref[0] * (conditional - unconditional)
    out_ref[...] = guided.astype(jnp.bfloat16)


def local_call(kernel, out_shape, in_spaces, arrays, scratch=()):
    out_spec = pl.BlockSpec(memory_space=pltpu.VMEM)
    return pl.pallas_call(
        kernel,
        out_shape=out_shape,
        in_specs=[pl.BlockSpec(memory_space=space) for space in in_spaces],
        out_specs=[out_spec] * len(out_shape) if isinstance(out_shape, list) else out_spec,
        scratch_shapes=scratch,
        compiler_params=pltpu.CompilerParams(vmem_limit_bytes=VMEM_LIMIT),
    )(
        *(
            pltpu.with_memory_space_constraint(array, space) if space == pltpu.HBM else array
            for array, space in zip(arrays, in_spaces)
        )
    )


def per_device(query_self, query_cross, key_vectors, values, positions, counts, guidance):
    n_tower, n_seq = lax.axis_size("tower"), lax.axis_size("seq")
    devices = n_tower * n_seq
    tokens, features = query_self.shape[1:]
    query_blocks = devices // HEADS
    block_rows = tokens // query_blocks
    video_keys = (n_tower - 1) * n_seq * tokens
    spreading, collecting = list(range(devices)), list(range(devices))
    if query_blocks == 1:
        spreading = spreading[-1:] + spreading[:-1]
        collecting = collecting[-1:] + collecting[:-1]
    ranks = [[order.index(device) for device in range(devices)] for order in (spreading, collecting)]

    def exchange(array, order):
        return lax.all_to_all(
            array,
            ("tower", "seq"),
            split_axis=0,
            concat_axis=0,
            tiled=True,
            axis_index_groups=[order],
        )

    packed, bias, kept_rows = local_call(
        functools.partial(rotate_kernel, video_keys),
        [
            pltpu.VMEM((HEADS, 4, tokens, DHEAD), jnp.bfloat16),
            pltpu.VMEM((2, devices * tokens), jnp.float32),
            pltpu.VMEM((devices * block_rows, DHEAD), jnp.float32),
        ],
        [pltpu.HBM] * 6,
        (positions, counts, query_self, query_cross, key_vectors, values),
        [
            pltpu.VMEM((4, tokens, features), jnp.bfloat16),
            pltpu.SMEM((tokens,), jnp.int32),
            pltpu.SMEM((devices,), jnp.int32),
            pltpu.SemaphoreType.DMA((6,)),
        ],
    )
    if query_blocks == 1:
        arrived = [exchange(packed, spreading)]
    else:
        queries = packed[:, :2].reshape(HEADS, 2, query_blocks, block_rows, DHEAD)
        queries = queries.transpose(0, 2, 1, 3, 4).reshape(devices, 2, block_rows, DHEAD)
        spread = jnp.broadcast_to(packed[:, None, 2:], (HEADS, query_blocks, 2, tokens, DHEAD))
        spread = spread.reshape(devices, 2, tokens, DHEAD)
        arrived = [
            exchange(part, spreading).transpose(1, 0, 2, 3).reshape(2, -1, DHEAD)
            for part in (queries, spread)
        ]
        arrived = [part[at] for part in arrived for at in range(2)]
    blocks = local_call(
        functools.partial(attend_kernel, n_tower, ranks),
        pltpu.VMEM((devices, block_rows, DHEAD), jnp.bfloat16),
        [pltpu.VMEM] * (2 + len(arrived)),
        (bias, kept_rows, *arrived),
    )
    half = (tokens, features // 2)
    returned = exchange(blocks, collecting).reshape(HEADS, tokens, DHEAD)
    workers = spreading if query_blocks == 1 else list(range(HEADS))
    kept, sent = local_call(
        functools.partial(norm_kernel, [ranks[1][worker] for worker in workers]),
        [pltpu.VMEM(half, jnp.bfloat16)] * 2,
        [pltpu.VMEM],
        (returned,),
    )
    met = lax.ppermute(sent, "cfg", [(0, 1), (1, 0)])
    return local_call(
        guide_kernel,
        jax.ShapeDtypeStruct(half, jnp.bfloat16),
        [pltpu.SMEM, pltpu.VMEM, pltpu.VMEM],
        (guidance, kept, met),
    )


def solution(mesh):
    return jax.shard_map(
        per_device,
        mesh=mesh,
        in_specs=(
            P("cfg", ("tower", "seq"), None),
            P("cfg", ("tower", "seq"), None),
            P("cfg", ("tower", "seq"), None),
            P("cfg", ("tower", "seq"), None),
            P(("tower", "seq")),
            P(),
            P(),
        ),
        out_specs=P(("tower", "seq"), "cfg"),
        check_vma=False,
    )
```

time: 95.9 us -> 29.6 us (0.31)
  starting transfers between devices: 20.3 us -> 0.07 us
  other arithmetic: 15.2 us -> 0 us
  waiting for transfers between devices: 12.8 us -> 0.55 us
  local copies, waits for them, and re-layouts: 11.9 us -> 0 us
  blocking collectives: 31.8 us -> 25.7 us
  Pallas kernels: 0 us -> 2.44 us
  matrix products: 1.89 us -> 0 us
    all_gather x2 -> x0, blocking collectives: 28 us -> none  [the longest x1 14.1 us: per_device(): lax.all_gather(rot_keys, 'tower', axis=0, tiled=True)]
    all_to_all x1 -> x2, blocking collectives: 3.79 us -> 25.7 us  [exchange(): lax.all_to_all(array, ('tower', 'seq'), split_axis=0, concat_axis=0, tile...]
    all_to_all x5 -> x0, starting transfers between devices: 20.3 us -> none  [the longest x1 5.16 us: per_device(): lax.all_to_all(spread_queries(rot_cross), 'seq', split_axis=0, concat_axi...]
    all_to_all x5 -> x0, waiting for transfers between devices: 12.8 us -> none  [the longest x1 5.25 us: per_device(): lax.all_to_all(spread_keys(value_source, towers_here), 'seq', split_axis=...]
    unnamed x7 -> x0, other arithmetic: 12.4 us -> none
    unnamed x20 -> x0, local copies, waits for them, and re-layouts: 4.76 us -> none
    transpose x4 -> x0, local copies, waits for them, and re-layouts: 2.76 us -> none  [the longest x2 1.5 us: spread_keys(): matrix.reshape(towers_here, tokens_here, groups, head_width)]
    pallas_call x0 -> x4, Pallas kernels: none -> 2.44 us  [local_call(): pl.pallas_call(kernel, out_shape=out_shape, in_specs=[pl.BlockSpec(memory...]
  transfers between devices with their start and end apart: 5 -> 1, of which waited for: 3 -> 1; matrix products, arithmetic and copies ran while one was open for 5% -> 0% of each run, Pallas kernels for 0% -> 0%
where the time goes in v1:
time: 29.6 us; the launch traced here: 29.4 us
  blocking collectives  25.7 us (87%)
  Pallas kernels  2.44 us (8%)
  between operations  0.68 us (2%)
  waiting for transfers between devices  0.55 us (2%)
    all_to_all x2, blocking collectives, exchange(): lax.all_to_all(array, ('tower', 'seq'), split_axis=0, concat_axis=0, tile...  25.7 us
    pallas_call x4, Pallas kernels, local_call(): pl.pallas_call(kernel, out_shape=out_shape, in_specs=[pl.BlockSpec(memory...  2.44 us
  transfers between devices with their start and end apart: 1, of which 1 were waited for; matrix products, arithmetic and copies ran while one was open for 0% of the time, Pallas kernels for 0%

profile of v1, /device:TPU:0, one launch (start us, length us, event | category | flops | bytes accessed | tf_op | source)
XLA Modules:
  0.0 29.4 jit_solution(9606703784304791812)
XLA Ops:
  0.0 1.2 %shard_map.73 = (bf16[16,4,16,128]{3,2,1,0:T(8,128)(2,1)S(1)}, f32[2,256]{1,0:T(2,128)S(1)}, f32[256,128]{1,0:T(8,128)S(1)}) custom-call(s32[16]{0:T(128)} %positions_hbm.1, s32[16]{0:T(128)} %counts_hbm.1, bf16[1,16,2048]{2,1,0:T(8,128)(2,1)} %refs_0_.1, bf16[1,16,2048]{2,1,0:T(8,128)(2,1)} %refs_1_.1, bf16[1,16,2048]{2,1,0:T(8,128)(2,1)} %refs_2_.1, ...), custom_call_target="tpu_custom_call" | custom-call | tf_op jit(solution)/shard_map/pallas_call | solution.py:141
  1.2 15.5 %all_to_all.10.refs_0_ = bf16[16,4,16,128]{3,2,1,0:T(8,128)(2,1)S(1)} all-to-all(bf16[16,4,16,128]{3,2,1,0:T(8,128)(2,1)S(1)} %get-tuple-element.12), channel_id=1, replica_groups={{15,0,1,2,3,4,5,6,7,8,9,10,11,12,13,14},{31,16,17,18,19,20,21,22,23,24,..., dimensions={0} | all-to-all | bytes 524288 | tf_op jit(solution)/shard_map/all_to_all | solution.py:170
  16.8 0.5 %shard_map.74 = bf16[16,16,128]{2,1,0:T(8,128)(2,1)S(1)} custom-call(f32[2,256]{1,0:T(2,128)S(1)} %get-tuple-element.10.bias_ref, f32[256,128]{1,0:T(8,128)S(1)} %get-tuple-element.11.kept_ref, bf16[16,4,16,128]{3,2,1,0:T(8,128)(2,1)S(1)} %all_to_all.10.refs_0_), custom_call_target="tpu_custom_call" | custom-call | tf_op jit(solution)/shard_map/pallas_call | solution.py:141
  17.3 10.1 %all_to_all.11.blocks_ref = bf16[16,16,128]{2,1,0:T(8,128)(2,1)S(1)} all-to-all(bf16[16,16,128]{2,1,0:T(8,128)(2,1)S(1)} %shard_map.74), channel_id=1, replica_groups={{15,0,1,2,3,4,5,6,7,8,9,10,11,12,13,14},{31,16,17,18,19,20,21,22,23,24,..., dimensions={0} | all-to-all | bytes 131072 | tf_op jit(solution)/shard_map/all_to_all | solution.py:170
  27.4 0.1 shard_map.75
  27.5 0.1 collective-permute-start
  28.2 0.5 %collective-permute-done.met_ref = bf16[16,1024]{1,0:T(8,128)(2,1)S(1)} collective-permute-done((bf16[16,1024]{1,0:T(8,128)(2,1)S(1)}, bf16[16,1024]{1,0:T(8,128)(2,1)S(1)}, u32[]{:S(2)}, u32[]{:S(2)}) %collective-permute-start) | collective-permute-done | bytes 32800 | tf_op jit(solution)/shard_map/ppermute | solution.py:222
  28.8 0.6 %shard_map.76 = bf16[16,1024]{1,0:T(8,128)(2,1)} custom-call(f32[1]{0:T(128)S(6)} %copy.8.guidance_ref, bf16[16,1024]{1,0:T(8,128)(2,1)S(1)} %get-tuple-element.13.kept_ref, bf16[16,1024]{1,0:T(8,128)(2,1)S(1)} %collective-permute-done.met_ref), custom_call_target="tpu_custom_call" | custom-call | tf_op jit(solution)/shard_map/pallas_call | solution.py:141
Async XLA Ops:
  27.5 1.3 %collective-permute-start = (bf16[16,1024]{1,0:T(8,128)(2,1)S(1)}, bf16[16,1024]{1,0:T(8,128)(2,1)S(1)}, u32[]{:S(2)}, u32[]{:S(2)}) collective-permute-start(bf16[16,1024]{1,0:T(8,128)(2,1)S(1)} %get-tuple-element.14), channel_id=1, source_target_pairs={{0,16},{16,0},{1,17},{17,1},{2,18},{18,2},{3,19},{19,3},{4,20},{20... | collective-permute-start | bytes 98312 | tf_op jit(solution)/shard_map/ppermute | solution.py:222

commit v2 on v1

--- a/solution.py
+++ b/solution.py
@@ -14,19 +14,37 @@
 VMEM_LIMIT = 32 * 1024 * 1024
 
 
+def sine_and_cosine(angles):
+    turns = jnp.floor(angles * (2.0 / math.pi) + 0.5)
+    rest = angles - turns * 1.5703125
+    rest = rest - turns * 4.837512969970703e-4
+    rest = rest - turns * 7.549789954891882e-8
+    square = rest * rest
+    sine = (-1.9515295891e-4 * square + 8.3321608736e-3) * square - 1.6666654611e-1
+    sine = rest + rest * square * sine
+    cosine = (2.443315711809948e-5 * square - 1.388731625493765e-3) * square
+    cosine = 1.0 - 0.5 * square + square * square * (cosine + 4.166664568298827e-2)
+    quarter = turns.astype(jnp.int32)
+    odd = (quarter & 1) == 1
+    sine, cosine = jnp.where(odd, cosine, sine), jnp.where(odd, sine, cosine)
+    sine = jnp.where((quarter & 2) == 2, -sine, sine)
+    cosine = jnp.where(((quarter + 1) & 2) == 2, -cosine, cosine)
+    return sine, cosine
+
+
 def rotate_kernel(video_keys, positions_hbm, counts_hbm, *refs):
     sources, (packed_ref, bias_ref, kept_ref) = refs[:4], refs[4:7]
     held, positions_ref, counts_ref, semaphores = refs[7:]
     tokens = held.shape[1]
-    copies = [pltpu.make_async_copy(positions_hbm, positions_ref, semaphores.at[4])]
-    for part in range(4):
-        copies.append(
-            pltpu.make_async_copy(sources[part].at[0], held.at[part], semaphores.at[part])
-        )
+    copies = [
+        pltpu.make_async_copy(sources[part].at[0], held.at[part], semaphores.at[part])
+        for part in range(4)
+    ]
+    copies.append(pltpu.make_async_copy(positions_hbm, positions_ref, semaphores.at[4]))
     copies.append(pltpu.make_async_copy(counts_hbm, counts_ref, semaphores.at[5]))
     for copy in copies:
         copy.start()
-    copies[0].wait()
+    copies[4].wait()
     row = lax.broadcasted_iota(jnp.int32, (tokens, DHEAD), 0)
     lane = lax.broadcasted_iota(jnp.int32, (tokens, DHEAD), 1)
     time = jnp.zeros((tokens, DHEAD), jnp.int32)
@@ -35,17 +53,17 @@
     half = DHEAD // 2
     index = (lane % half).astype(jnp.float32)
     angles = time.astype(jnp.float32) * jnp.exp(index * (-2.0 * math.log(10000.0) / DHEAD))
-    cosine = jnp.cos(angles)
-    sine = jnp.where(lane < half, -jnp.sin(angles), jnp.sin(angles))
+    sine, cosine = sine_and_cosine(angles)
+    sine = jnp.where(lane < half, -sine, sine)
+    for copy in copies[:4] + copies[5:]:
+        copy.wait()
     for part in range(4):
-        copies[1 + part].wait()
         for head in range(HEADS):
             columns = held[part, :, head * DHEAD : (head + 1) * DHEAD]
             if part < 3:
                 columns = columns.astype(jnp.float32)
                 columns = columns * cosine + pltpu.roll(columns, half, 1) * sine
-            packed_ref[head, part] = columns.astype(jnp.bfloat16)
-    copies[5].wait()
+            packed_ref[head, part * tokens : (part + 1) * tokens] = columns.astype(jnp.bfloat16)
     devices = counts_ref.shape[0]
     limits = [counts_ref[device] for device in range(devices)]
     key = lax.broadcasted_iota(jnp.int32, bias_ref.shape, 1)
@@ -85,7 +103,10 @@
     devices, block_rows, _ = out_ref.shape
     if len(refs) == 2:
         q_self, q_cross, keys, values = (
-            jnp.concatenate([refs[0][rank, part] for rank in ranks[0]], axis=0)
+            jnp.concatenate(
+                [refs[0][rank, part * block_rows : (part + 1) * block_rows] for rank in ranks[0]],
+                axis=0,
+            )
             for part in range(4)
         )
     else:
@@ -162,8 +183,9 @@
     video_keys = (n_tower - 1) * n_seq * tokens
     spreading, collecting = list(range(devices)), list(range(devices))
     if query_blocks == 1:
-        spreading = spreading[-1:] + spreading[:-1]
-        collecting = collecting[-1:] + collecting[:-1]
+        spreading.reverse()
+        middle = devices - n_seq - 1
+        collecting = collecting[middle:] + collecting[:middle]
     ranks = [[order.index(device) for device in range(devices)] for order in (spreading, collecting)]
 
     def exchange(array, order):
@@ -179,7 +201,7 @@
     packed, bias, kept_rows = local_call(
         functools.partial(rotate_kernel, video_keys),
         [
-            pltpu.VMEM((HEADS, 4, tokens, DHEAD), jnp.bfloat16),
+            pltpu.VMEM((HEADS, 4 * tokens, DHEAD), jnp.bfloat16),
             pltpu.VMEM((2, devices * tokens), jnp.float32),
             pltpu.VMEM((devices * block_rows, DHEAD), jnp.float32),
         ],
@@ -195,6 +217,7 @@
     if query_blocks == 1:
         arrived = [exchange(packed, spreading)]
     else:
+        packed = packed.reshape(HEADS, 4, tokens, DHEAD)
         queries = packed[:, :2].reshape(HEADS, 2, query_blocks, block_rows, DHEAD)
         queries = queries.transpose(0, 2, 1, 3, 4).reshape(devices, 2, block_rows, DHEAD)
         spread = jnp.broadcast_to(packed[:, None, 2:], (HEADS, query_blocks, 2, tokens, DHEAD))

time: 29.6 us -> 29.6 us (level)
  no operation moved by 1% of the time
where the time goes in v2:
time: 29.6 us; the launch traced here: 29.3 us
  blocking collectives  25.7 us (87%)
  Pallas kernels  2.36 us (8%)
  between operations  0.68 us (2%)
  waiting for transfers between devices  0.55 us (2%)
    all_to_all x2, blocking collectives, exchange(): lax.all_to_all(array, ('tower', 'seq'), split_axis=0, concat_axis=0, tile...  25.7 us
    pallas_call x4, Pallas kernels, local_call(): pl.pallas_call(kernel, out_shape=out_shape, in_specs=[pl.BlockSpec(memory...  2.36 us
  transfers between devices with their start and end apart: 1, of which 1 were waited for; matrix products, arithmetic and copies ran while one was open for 0% of the time, Pallas kernels for 0%

profile of v2, /device:TPU:0, one launch (start us, length us, event | category | flops | bytes accessed | tf_op | source)
XLA Modules:
  0.0 29.3 jit_solution(8284839858441180830)
XLA Ops:
  0.0 1.1 %shard_map.73 = (bf16[16,64,128]{2,1,0:T(8,128)(2,1)S(1)}, f32[2,256]{1,0:T(2,128)S(1)}, f32[256,128]{1,0:T(8,128)S(1)}) custom-call(s32[16]{0:T(128)} %positions_hbm.1, s32[16]{0:T(128)} %counts_hbm.1, bf16[1,16,2048]{2,1,0:T(8,128)(2,1)} %refs_0_.1, bf16[1,16,2048]{2,1,0:T(8,128)(2,1)} %refs_1_.1, bf16[1,16,2048]{2,1,0:T(8,128)(2,1)} %refs_2_.1, ...), custom_call_target="tpu_custom_call" | custom-call | tf_op jit(solution)/shard_map/pallas_call | solution.py:162
  1.1 16.2 %all_to_all.10.refs_0_ = bf16[16,64,128]{2,1,0:T(8,128)(2,1)S(1)} all-to-all(bf16[16,64,128]{2,1,0:T(8,128)(2,1)S(1)} %get-tuple-element.12), channel_id=1, replica_groups={{15,14,13,12,11,10,9,8,7,6,5,4,3,2,1,0},{31,30,29,28,27,26,25,24,23,22,..., dimensions={0} | all-to-all | bytes 524288 | tf_op jit(solution)/shard_map/all_to_all | solution.py:192
  17.3 0.5 %shard_map.74 = bf16[16,16,128]{2,1,0:T(8,128)(2,1)S(1)} custom-call(f32[2,256]{1,0:T(2,128)S(1)} %get-tuple-element.10.bias_ref, f32[256,128]{1,0:T(8,128)S(1)} %get-tuple-element.11.kept_ref, bf16[16,64,128]{2,1,0:T(8,128)(2,1)S(1)} %all_to_all.10.refs_0_), custom_call_target="tpu_custom_call" | custom-call | tf_op jit(solution)/shard_map/pallas_call | solution.py:162
  17.8 9.5 %all_to_all.11.blocks_ref = bf16[16,16,128]{2,1,0:T(8,128)(2,1)S(1)} all-to-all(bf16[16,16,128]{2,1,0:T(8,128)(2,1)S(1)} %shard_map.74), channel_id=1, replica_groups={{11,12,13,14,15,0,1,2,3,4,5,6,7,8,9,10},{27,28,29,30,31,16,17,18,19,20,..., dimensions={0} | all-to-all | bytes 131072 | tf_op jit(solution)/shard_map/all_to_all | solution.py:192
  27.3 0.1 shard_map.75
  27.4 0.1 collective-permute-start
  28.2 0.5 %collective-permute-done.met_ref = bf16[16,1024]{1,0:T(8,128)(2,1)S(1)} collective-permute-done((bf16[16,1024]{1,0:T(8,128)(2,1)S(1)}, bf16[16,1024]{1,0:T(8,128)(2,1)S(1)}, u32[]{:S(2)}, u32[]{:S(2)}) %collective-permute-start) | collective-permute-done | bytes 32800 | tf_op jit(solution)/shard_map/ppermute | solution.py:245
  28.7 0.6 %shard_map.76 = bf16[16,1024]{1,0:T(8,128)(2,1)} custom-call(f32[1]{0:T(128)S(6)} %copy.8.guidance_ref, bf16[16,1024]{1,0:T(8,128)(2,1)S(1)} %get-tuple-element.13.kept_ref, bf16[16,1024]{1,0:T(8,128)(2,1)S(1)} %collective-permute-done.met_ref), custom_call_target="tpu_custom_call" | custom-call | tf_op jit(solution)/shard_map/pallas_call | solution.py:162
Async XLA Ops:
  27.4 1.3 %collective-permute-start = (bf16[16,1024]{1,0:T(8,128)(2,1)S(1)}, bf16[16,1024]{1,0:T(8,128)(2,1)S(1)}, u32[]{:S(2)}, u32[]{:S(2)}) collective-permute-start(bf16[16,1024]{1,0:T(8,128)(2,1)S(1)} %get-tuple-element.14), channel_id=1, source_target_pairs={{0,16},{16,0},{1,17},{17,1},{2,18},{18,2},{3,19},{19,3},{4,20},{20... | collective-permute-start | bytes 98312 | tf_op jit(solution)/shard_map/ppermute | solution.py:245

commit v3 on v2

--- a/solution.py
+++ b/solution.py
@@ -12,24 +12,6 @@
 DHEAD = 128
 EXPONENT_SCALE = math.log2(math.e) / math.sqrt(DHEAD)
 VMEM_LIMIT = 32 * 1024 * 1024
-
-
-def sine_and_cosine(angles):
-    turns = jnp.floor(angles * (2.0 / math.pi) + 0.5)
-    rest = angles - turns * 1.5703125
-    rest = rest - turns * 4.837512969970703e-4
-    rest = rest - turns * 7.549789954891882e-8
-    square = rest * rest
-    sine = (-1.9515295891e-4 * square + 8.3321608736e-3) * square - 1.6666654611e-1
-    sine = rest + rest * square * sine
-    cosine = (2.443315711809948e-5 * square - 1.388731625493765e-3) * square
-    cosine = 1.0 - 0.5 * square + square * square * (cosine + 4.166664568298827e-2)
-    quarter = turns.astype(jnp.int32)
-    odd = (quarter & 1) == 1
-    sine, cosine = jnp.where(odd, cosine, sine), jnp.where(odd, sine, cosine)
-    sine = jnp.where((quarter & 2) == 2, -sine, sine)
-    cosine = jnp.where(((quarter + 1) & 2) == 2, -cosine, cosine)
-    return sine, cosine
 
 
 def rotate_kernel(video_keys, positions_hbm, counts_hbm, *refs):
@@ -53,8 +35,8 @@
     half = DHEAD // 2
     index = (lane % half).astype(jnp.float32)
     angles = time.astype(jnp.float32) * jnp.exp(index * (-2.0 * math.log(10000.0) / DHEAD))
-    sine, cosine = sine_and_cosine(angles)
-    sine = jnp.where(lane < half, -sine, sine)
+    cosine = jnp.cos(angles)
+    sine = jnp.where(lane < half, -jnp.sin(angles), jnp.sin(angles))
     for copy in copies[:4] + copies[5:]:
         copy.wait()
     for part in range(4):
@@ -129,32 +111,42 @@
         out_ref[ranks[1][device]] = combined[device * block_rows : (device + 1) * block_rows]
 
 
-def norm_kernel(head_ranks, blocks_ref, kept_ref, sent_ref):
+def norm_scale(blocks_ref):
     heads, tokens, _ = blocks_ref.shape
-    half_heads = heads // 2
-    core = lax.axis_index("cfg")
     total = jnp.zeros((tokens, DHEAD), jnp.float32)
     for head in range(heads):
         block = blocks_ref[head].astype(jnp.float32)
         total += block * block
     mean = jnp.sum(total, axis=1, keepdims=True) * (1.0 / (heads * DHEAD))
-    scale = lax.rsqrt(mean + 1e-6)
-    for at in range(half_heads):
-        low, high = head_ranks[at], head_ranks[half_heads + at]
-        for rank, target in (
-            (jnp.where(core == 0, low, high), kept_ref),
-            (jnp.where(core == 0, high, low), sent_ref),
-        ):
-            normed = blocks_ref[rank].astype(jnp.float32) * scale
-            target[:, at * DHEAD : (at + 1) * DHEAD] = normed.astype(jnp.bfloat16)
-
-
-def guide_kernel(guidance_ref, kept_ref, met_ref, out_ref):
-    kept, met = kept_ref[...].astype(jnp.float32), met_ref[...].astype(jnp.float32)
+    return lax.rsqrt(mean + 1e-6)
+
+
+def half_ranks(head_ranks):
+    half_heads = len(head_ranks) // 2
     first = lax.axis_index("cfg") == 0
-    conditional, unconditional = jnp.where(first, kept, met), jnp.where(first, met, kept)
-    guided = unconditional + guidance_ref[0] * (conditional - unconditional)
-    out_ref[...] = guided.astype(jnp.bfloat16)
+    return [
+        jnp.where(first, head_ranks[at], head_ranks[half_heads + at]) for at in range(half_heads)
+    ]
+
+
+def norm_kernel(head_ranks, blocks_ref, kept_ref):
+    scale = norm_scale(blocks_ref)
+    for at, rank in enumerate(half_ranks(head_ranks)):
+        normed = blocks_ref[rank].astype(jnp.float32) * scale
+        kept_ref[:, at * DHEAD : (at + 1) * DHEAD] = normed.astype(jnp.bfloat16)
+
+
+def guide_kernel(head_ranks, guidance_ref, kept_ref, met_ref, out_ref):
+    scale = norm_scale(met_ref)
+    first = lax.axis_index("cfg") == 0
+    guidance = guidance_ref[0]
+    for at, rank in enumerate(half_ranks(head_ranks)):
+        columns = slice(at * DHEAD, (at + 1) * DHEAD)
+        kept = kept_ref[:, columns].astype(jnp.float32)
+        met = (met_ref[rank].astype(jnp.float32) * scale).astype(jnp.bfloat16).astype(jnp.float32)
+        conditional, unconditional = jnp.where(first, kept, met), jnp.where(first, met, kept)
+        guided = unconditional + guidance * (conditional - unconditional)
+        out_ref[:, columns] = guided.astype(jnp.bfloat16)
 
 
 def local_call(kernel, out_shape, in_spaces, arrays, scratch=()):
@@ -183,9 +175,9 @@
     video_keys = (n_tower - 1) * n_seq * tokens
     spreading, collecting = list(range(devices)), list(range(devices))
     if query_blocks == 1:
-        spreading.reverse()
+        spreading = [devices - 1 - at // 2 if at % 2 == 0 else at // 2 for at in range(devices)]
         middle = devices - n_seq - 1
-        collecting = collecting[middle:] + collecting[:middle]
+        collecting = [middle] + [device for device in spreading if device != middle]
     ranks = [[order.index(device) for device in range(devices)] for order in (spreading, collecting)]
 
     def exchange(array, order):
@@ -236,15 +228,16 @@
     half = (tokens, features // 2)
     returned = exchange(blocks, collecting).reshape(HEADS, tokens, DHEAD)
     workers = spreading if query_blocks == 1 else list(range(HEADS))
-    kept, sent = local_call(
-        functools.partial(norm_kernel, [ranks[1][worker] for worker in workers]),
-        [pltpu.VMEM(half, jnp.bfloat16)] * 2,
+    head_ranks = [ranks[1][worker] for worker in workers]
+    met = lax.ppermute(returned, "cfg", [(0, 1), (1, 0)])
+    kept = local_call(
+        functools.partial(norm_kernel, head_ranks),
+        pltpu.VMEM(half, jnp.bfloat16),
         [pltpu.VMEM],
         (returned,),
     )
-    met = lax.ppermute(sent, "cfg", [(0, 1), (1, 0)])
     return local_call(
-        guide_kernel,
+        functools.partial(guide_kernel, head_ranks),
         jax.ShapeDtypeStruct(half, jnp.bfloat16),
         [pltpu.SMEM, pltpu.VMEM, pltpu.VMEM],
         (guidance, kept, met),

time: 29.6 us -> 29.5 us (level)
  no operation moved by 1% of the time
where the time goes in v3:
time: 29.5 us; the launch traced here: 29.2 us
  blocking collectives  25.6 us (87%)
  Pallas kernels  2.45 us (8%)
  between operations  0.67 us (2%)
  waiting for transfers between devices  0.49 us (2%)
    all_to_all x2, blocking collectives, exchange(): lax.all_to_all(array, ('tower', 'seq'), split_axis=0, concat_axis=0, tile...  25.6 us
    pallas_call x4, Pallas kernels, local_call(): pl.pallas_call(kernel, out_shape=out_shape, in_specs=[pl.BlockSpec(memory...  2.45 us
  transfers between devices with their start and end apart: 1, of which 1 were waited for; matrix products, arithmetic and copies ran while one was open for 0% of the time, Pallas kernels for 0%

profile of v3, /device:TPU:0, one launch (start us, length us, event | category | flops | bytes accessed | tf_op | source)
XLA Modules:
  0.0 29.2 jit_solution(13108929532812997199)
XLA Ops:
  0.0 1.1 %shard_map.73 = (bf16[16,64,128]{2,1,0:T(8,128)(2,1)S(1)}, f32[2,256]{1,0:T(2,128)S(1)}, f32[256,128]{1,0:T(8,128)S(1)}) custom-call(s32[16]{0:T(128)} %positions_hbm.1, s32[16]{0:T(128)} %counts_hbm.1, bf16[1,16,2048]{2,1,0:T(8,128)(2,1)} %refs_0_.1, bf16[1,16,2048]{2,1,0:T(8,128)(2,1)} %refs_1_.1, bf16[1,16,2048]{2,1,0:T(8,128)(2,1)} %refs_2_.1, ...), custom_call_target="tpu_custom_call" | custom-call | tf_op jit(solution)/shard_map/pallas_call | solution.py:154
  1.1 15.7 %all_to_all.10.refs_0_ = bf16[16,64,128]{2,1,0:T(8,128)(2,1)S(1)} all-to-all(bf16[16,64,128]{2,1,0:T(8,128)(2,1)S(1)} %get-tuple-element.10), channel_id=1, replica_groups={{15,0,14,1,13,2,12,3,11,4,10,5,9,6,8,7},{31,16,30,17,29,18,28,19,27,20,..., dimensions={0} | all-to-all | bytes 524288 | tf_op jit(solution)/shard_map/all_to_all | solution.py:184
  16.8 0.5 %shard_map.74 = bf16[16,16,128]{2,1,0:T(8,128)(2,1)S(1)} custom-call(f32[2,256]{1,0:T(2,128)S(1)} %get-tuple-element.8.bias_ref, f32[256,128]{1,0:T(8,128)S(1)} %get-tuple-element.9.kept_ref, bf16[16,64,128]{2,1,0:T(8,128)(2,1)S(1)} %all_to_all.10.refs_0_), custom_call_target="tpu_custom_call" | custom-call | tf_op jit(solution)/shard_map/pallas_call | solution.py:154
  17.3 9.9 %all_to_all.11.blocks_ref = bf16[16,16,128]{2,1,0:T(8,128)(2,1)S(1)} all-to-all(bf16[16,16,128]{2,1,0:T(8,128)(2,1)S(1)} %shard_map.74), channel_id=1, replica_groups={{11,15,0,14,1,13,2,12,3,4,10,5,9,6,8,7},{27,31,16,30,17,29,18,28,19,20,..., dimensions={0} | all-to-all | bytes 131072 | tf_op jit(solution)/shard_map/all_to_all | solution.py:184
  27.2 0.0 collective-permute-start
  27.9 0.1 shard_map.75.kept_ref
  28.0 0.5 %collective-permute-done.met_ref = bf16[16,16,128]{2,1,0:T(8,128)(2,1)S(1)} collective-permute-done((bf16[16,16,128]{2,1,0:T(8,128)(2,1)S(1)}, bf16[16,16,128]{2,1,0:T(8,128)(2,1)S(1)}, u32[]{:S(2)}, u32[]{:S(2)}) %collective-permute-start) | collective-permute-done | bytes 65568 | tf_op jit(solution)/shard_map/ppermute | solution.py:232
  28.5 0.7 %shard_map.76 = bf16[16,1024]{1,0:T(8,128)(2,1)} custom-call(f32[1]{0:T(128)S(6)} %copy.8.guidance_ref, bf16[16,1024]{1,0:T(8,128)(2,1)S(1)} %shard_map.75.kept_ref, bf16[16,16,128]{2,1,0:T(8,128)(2,1)S(1)} %collective-permute-done.met_ref), custom_call_target="tpu_custom_call" | custom-call | tf_op jit(solution)/shard_map/pallas_call | solution.py:154
Async XLA Ops:
  27.2 1.3 %collective-permute-start = (bf16[16,16,128]{2,1,0:T(8,128)(2,1)S(1)}, bf16[16,16,128]{2,1,0:T(8,128)(2,1)S(1)}, u32[]{:S(2)}, u32[]{:S(2)}) collective-permute-start(bf16[16,16,128]{2,1,0:T(8,128)(2,1)S(1)} %all_to_all.11.blocks_ref), channel_id=1, source_target_pairs={{0,16},{16,0},{1,17},{17,1},{2,18},{18,2},{3,19},{19,3},{4,20},{20... | collective-permute-start | bytes 196616 | tf_op jit(solution)/shard_map/ppermute | solution.py:232
